TPU v7x, 32 devices: a whole 2x2x4 slice. The times are simulated.
32 devices in a mesh: grp: 4 (over y, x), row: 8 (over z, core).
Axes of the slice: x: 2, y: 2, z: 4, core: 2. Of those that a mesh axis runs over, the one named last changes fastest.
Arguments:
- field: float32 [4, 16, 512, 512], P(None, 'grp', None, 'row'), may hold values from -200 to 200
Outputs:
- factor: float32 [512, 512], replicated
- orthonormal: float32 [4, 16, 512, 512], P(None, 'grp', 'row')
All inputs are finite; a program needn't handle non-finite values.
Results may differ from a plain program's by a relative error of at most 0.000073.
Values sent between devices are 32-bit elements; how exact they have to be, the bound alone decides.
A program may use at most 128 MiB of HBM per device.

v0:
```python
import jax
import jax.numpy as jnp
from jax import lax
from jax.sharding import PartitionSpec as P


def block_grams(pieces):
    mats = pieces.reshape(pieces.shape[0], -1, pieces.shape[-1])
    grams = jnp.einsum(
        "fcn,fcm->fnm",
        mats,
        mats,
        precision=lax.Precision.HIGHEST,
        preferred_element_type=jnp.float32,
    )
    return (pieces, grams)


def per_device(field):
    count = field.shape[0] * field.shape[1] * lax.axis_size("grp") * field.shape[2]
    scale = 1.0 / count
    slab, grams = block_grams(lax.all_to_all(field, "row", split_axis=2, concat_axis=3, tiled=True))
    gram = jnp.sum(grams, axis=0)
    total = lax.psum(gram, ("grp", "row"))
    factor = jnp.linalg.cholesky(total * scale)
    first = slab.shape[-1]
    solved = lax.linalg.triangular_solve(
        factor, slab.reshape(-1, first), left_side=False, lower=True, transpose_a=True
    )
    return (factor, solved.reshape(slab.shape))


def solution(mesh):
    placed = (P(None, "grp", None, "row"),)
    return jax.shard_map(
        per_device,
        mesh=mesh,
        in_specs=placed,
        out_specs=(P(), P(None, "grp", "row", None)),
        check_vma=False,
    )
```

profile of v0, /device:TPU:0, one launch (start us, length us, event | category | flops | bytes accessed | tf_op | source)
XLA Modules:
  0.0 411.9 jit_solution(6683738769054496946)
XLA Ops:
  7.2 4.9 %copy.13 = f32[4,4,512,64]{3,1,0,2:T(4,128)} copy(f32[4,4,512,64]{2,3,1,0:T(8,128)} %param.1) | data formatting | bytes 4194304 | tf_op args[0]
  12.1 6.8 %reshape.73 = f32[8,1,65536]{2,1,0:T(1,128)S(1)} reshape(f32[512,4,4,64]{3,2,1,0:T(4,128)} %bitcast.66) | data formatting | bytes 4194304
  18.9 55.3 %all_to_all.15 = f32[8,1,65536]{2,1,0:T(1,128)} all-to-all(f32[8,1,65536]{2,1,0:T(1,128)S(1)} %reshape.73), channel_id=1, replica_groups=mesh['grp'=4,'row'=8] {'row'}, dimensions={0} | all-to-all | bytes 4194304 | tf_op jit(solution)/shard_map/all_to_all | solution.py:22
  74.7 7.2 %reduce.24 = f32[8,65536]{1,0:T(8,128)S(1)} reduce(f32[8,1,65536]{2,1,0:T(1,128)} %all_to_all.15, f32[]{:T(128)} %broadcast.191), dimensions={1}, to_apply=%all_to_all.11.reduce_sub_computation | reduce | bytes 4194308 | tf_op jit(solution)/shard_map/all_to_all | solution.py:22
  81.9 4.8 %reshape.74 = f32[512,4,4,64]{3,2,1,0:T(4,128)} reshape(f32[8,65536]{1,0:T(8,128)S(1)} %reduce.24) | data formatting | bytes 4194304
  86.8 6.5 %copy.23 = f32[4,4,8,64,64]{4,2,3,1,0:T(8,128)} copy(f32[4,4,8,64,64]{4,1,0,3,2:T(4,128)} %bitcast.67) | data formatting | bytes 4194304 | tf_op jit(solution)/shard_map/all_to_all | solution.py:22
  93.3 15.0 %reshape.50 = f32[4,256,512]{2,1,0:T(8,128)S(1)} reshape(f32[4,4,64,8,64]{4,3,2,1,0:T(8,128)} %bitcast.64) | data formatting | bytes 4194304 | tf_op jit(solution)/shard_map/reshape | solution.py:8
  108.3 4.5 %convolution_bitcast_fusion = f32[512,512]{0,1:T(8,128)} fusion(f32[4,256,512]{2,1,0:T(8,128)S(1)} %reshape.50), kind=kOutput, calls=%fused_computation.10 | convolution fusion | flops 3221225472 | bytes 3145728 | tf_op jit(solution)/shard_map/fcn,fcm->fnm/dot_general | solution.py:9
  112.9 3.4 reshape.51
  116.3 125.4 %all-reduce.3.cloned.1.call-done = f32[512,512]{0,1:T(8,128)} async-done(((f32[512,512]{0,1:T(8,128)}), f32[512,512]{0,1:T(8,128)}) %all-reduce.3.cloned.1.call-update) | async-done | bytes 1048592 | tf_op jit(solution)/shard_map/psum | solution.py:24
  241.7 2.4 broadcast_multiply_fusion
  244.1 2.5 copy.17
  246.6 1.5 fusion.12
  249.1 11.7 %cholesky.104 = f32[128,128]{1,0:T(8,128)S(1)} custom-call(f32[128,128]{1,0:T(8,128)S(1)} %cholesky.266), custom_call_target="Cholesky" | custom-call | tf_op jit(solution)/shard_map/jit(cholesky)/cholesky | solution.py:25
  261.0 9.8 %custom-call.30 = f32[1,128,128]{1,2,0:T(8,128)S(1)} custom-call(f32[1,128,128]{2,1,0:T(8,128)S(1)} %get-tuple-element.33), custom_call_target="InvertDiagBlocksLowerTriangular" | custom-call | tf_op jit(solution)/shard_map/jit(cholesky)/cholesky | solution.py:25
  273.3 11.7 %cholesky.217 = f32[128,128]{1,0:T(8,128)S(1)} custom-call(f32[128,128]{1,0:T(8,128)S(1)} %cholesky.270), custom_call_target="Cholesky" | custom-call | tf_op jit(solution)/shard_map/jit(cholesky)/cholesky | solution.py:25
  285.1 10.2 %custom-call.31 = f32[1,128,128]{1,2,0:T(8,128)S(1)} custom-call(f32[1,128,128]{2,1,0:T(8,128)S(1)} %get-tuple-element.30), custom_call_target="InvertDiagBlocksLowerTriangular" | custom-call | tf_op jit(solution)/shard_map/jit(cholesky)/cholesky | solution.py:25
  295.5 1.3 convolution_subtract_fusion.3
  296.8 11.7 %cholesky.238 = f32[128,128]{1,0:T(8,128)S(1)} custom-call(f32[128,128]{1,0:T(8,128)S(1)} %cholesky.275), custom_call_target="Cholesky" | custom-call | tf_op jit(solution)/shard_map/jit(cholesky)/cholesky | solution.py:25
  308.6 9.8 %custom-call.32 = f32[1,128,128]{1,2,0:T(8,128)S(1)} custom-call(f32[1,128,128]{2,1,0:T(8,128)S(1)} %get-tuple-element.27), custom_call_target="InvertDiagBlocksLowerTriangular" | custom-call | tf_op jit(solution)/shard_map/jit(cholesky)/cholesky | solution.py:25
  319.8 11.7 %cholesky.255 = f32[128,128]{1,0:T(8,128)S(1)} custom-call(f32[128,128]{1,0:T(8,128)S(1)} %convolution_subtract_fusion.4), custom_call_target="Cholesky" | custom-call | tf_op jit(solution)/shard_map/jit(cholesky)/cholesky | solution.py:25
  336.3 1.6 fusion.13
  337.9 14.1 %while.1 = (s32[]{:T(128)}, f32[512,512]{1,0:T(8,128)}, s32[4,2]{0,1:T(2,128)S(1)}, f32[4,128,128]{2,1,0:T(8,128)}, s32[]{:T(128)}) while((s32[]{:T(128)}, f32[512,512]{1,0:T(8,128)}, s32[4,2]{0,1:T(2,128)S(1)}, f32[4,128,128]{2,1,0:T(8,128)}, s32[]{:T(128)}) %tuple.33), condition=%wide.while_cond, body=%wide.while_body.sunk | while | flops 2 | bytes 132205 | solution.py:27
  338.5 2.9 bitcast_dynamic-update-slice_fusion.2
  342.1 2.9 bitcast_dynamic-update-slice_fusion.2
  345.6 2.9 bitcast_dynamic-update-slice_fusion.2
  349.2 2.8 bitcast_dynamic-update-slice_fusion.2
  352.0 40.1 %custom-call.33 = f32[4,128,128]{1,2,0:T(8,128)S(1)} custom-call(f32[4,128,128]{2,1,0:T(8,128)} %get-tuple-element.9), custom_call_target="InvertDiagBlocksLowerTriangular" | custom-call | tf_op jit(solution)/shard_map/triangular_solve | solution.py:27
  392.7 1.8 convolution_subtract_fusion.1
  395.2 2.8 convolution_subtract_fusion
  398.6 3.7 fusion.6
  403.1 1.8 copy.18
  (39 shorter events, 13.5 us)
Async XLA Ops:
  7.2 234.6 %all-reduce.3.cloned.1.call-start = ((), (), s32[]{:S(2)}) async-start(), calls=%async_computation.1 | async-start | bytes 2097152 | tf_op jit(solution)/shard_map/psum | solution.py:24
  241.7 4.9 %copy-start = (f32[512,512]{0,1:T(8,128)S(1)}, f32[512,512]{0,1:T(8,128)}, u32[]{:S(2)}) copy-start(f32[512,512]{0,1:T(8,128)} %all-reduce.3.cloned.1.call-done) | copy-start | bytes 3145732
  248.1 1.0 copy-start.1
Sparse Core Ops, SparseCore 0:
  113.0 128.7 all-reduce.2
where the time goes:
time: 416 us; the launch traced here: 412 us
  other arithmetic  132 us (32%)
  waiting for transfers between devices  125 us (30%)
  local copies, waits for them, and re-layouts  61.6 us (15%)
  blocking collectives  55.3 us (13%)
  matrix products  20.8 us (5%)
  between operations  17 us (4%)
    psum x1, waiting for transfers between devices, per_device(): total = lax.psum(gram, ('grp', 'row'))  125 us
    another operation x14, other arithmetic, per_device(): factor = jnp.linalg.cholesky(total * scale)  78.9 us
    all_to_all x1, blocking collectives, per_device(): lax.all_to_all(field, 'row', split_axis=2, concat_axis=3, tiled=True)  55.3 us
    another operation x4, other arithmetic, per_device(): lax.linalg.triangular_solve(factor, slab.reshape(-1, first), left_side=Fa...  41.8 us
    unnamed x7, local copies, waits for them, and re-layouts  17.5 us
    reshape x1, local copies, waits for them, and re-layouts, block_grams(): mats = pieces.reshape(pieces.shape[0], -1, pieces.shape[-1])  15 us
    another operation x12, local copies, waits for them, and re-layouts  14.1 us
    another operation x7, matrix products, per_device(): lax.linalg.triangular_solve(factor, slab.reshape(-1, first), left_side=Fa...  10.8 us
  transfers between devices with their start and end apart: 1, of which 1 were waited for; matrix products, arithmetic and copies ran while one was open for 1% of the time, Pallas kernels for 0%

commit v1 on v0

v1 whole, which is shorter than its diff:
```python
import functools

import jax
import jax.numpy as jnp
from jax import lax
from jax.experimental import pallas as pl
from jax.experimental.pallas import tpu as pltpu
from jax.sharding import PartitionSpec as P

MESH = pl.DeviceIdType.MESH
LANES = 128
HIGHEST = lax.Precision.HIGHEST
NT = (((1,), (1,)), ((), ()))


def offsets(order):
    blocks = order // LANES
    starts, at = [], 0
    for j in range(blocks):
        starts.append(at)
        at += order - j * LANES
    return starts, at


def share_kernel(
    n_row, n_grp, n_chunk, scale,
    field_ref, xt_ref, total_ref,
    send_ref, x_ref, gram_ref, pair_ref, half_ref, grp_ref, z_ref, sum_ref,
    a2a_send, a2a_recv, pair_sems, grp_send, grp_recv, z_send, z_recv, back_send, back_recv,
):
    row = lax.axis_index("row")
    grp = lax.axis_index("grp")
    core = lax.rem(row, 2)
    z = row // 2
    n_z = n_row // 2
    count, depth, width = field_ref.shape
    piece = width // n_row
    per_tile = LANES // piece
    order, columns = x_ref.shape
    chunk = columns // n_chunk
    tiles = chunk // LANES
    starts, used = offsets(order)

    barrier = pltpu.get_barrier_semaphore()
    for s in range(1, n_row):
        pl.semaphore_signal(
            barrier, inc=1, device_id={"row": lax.rem(row + s, n_row)}, device_id_type=MESH
        )
    for s in range(1, n_grp):
        pl.semaphore_signal(
            barrier, inc=1, device_id={"grp": lax.rem(grp + s, n_grp)}, device_id_type=MESH
        )

    lane = lax.broadcasted_iota(jnp.int32, (depth, LANES), 1)

    def pack(k):
        for d in range(n_row):
            source = d * piece // LANES * LANES
            shift = d * piece % LANES
            for t in range(k * tiles, (k + 1) * tiles):
                packed = None
                for j in range(per_tile):
                    value = field_ref[t * per_tile + j, :, source:source + LANES]
                    turn = (j * piece - shift) % LANES
                    if turn:
                        value = pltpu.roll(value, turn, 1)
                    packed = value if packed is None else jnp.where(lane >= j * piece, value, packed)
                send_ref[d, :, t * LANES:(t + 1) * LANES] = packed

    def a2a(k, s):
        to = lax.rem(row + s, n_row)
        return pltpu.make_async_remote_copy(
            src_ref=send_ref.at[to, :, pl.ds(k * chunk, chunk)],
            dst_ref=x_ref.at[pl.ds(pl.multiple_of(row * depth, depth), depth), pl.ds(k * chunk, chunk)],
            send_sem=a2a_send.at[k, s],
            recv_sem=a2a_recv.at[k, s],
            device_id={"row": to},
            device_id_type=MESH,
        )

    steps = list(range(1, n_row))
    for k in range(n_chunk):
        pack(k)
        if k == 0:
            pl.semaphore_wait(barrier, n_row + n_grp - 2)
        for s in steps:
            a2a(k, s).start()
    x_ref[pl.ds(pl.multiple_of(row * depth, depth), depth), :] = send_ref[row]

    for k in range(n_chunk):
        for s in steps:
            a2a(k, s).wait_recv()
        for j, start in enumerate(starts):
            rows = order - j * LANES
            product = lax.dot_general(
                x_ref[j * LANES:, k * chunk:(k + 1) * chunk],
                x_ref[j * LANES:(j + 1) * LANES, k * chunk:(k + 1) * chunk],
                NT, precision=HIGHEST, preferred_element_type=jnp.float32,
            )
            if k == 0:
                gram_ref[start:start + rows, :] = product
            else:
                gram_ref[start:start + rows, :] += product

    if used < gram_ref.shape[0]:
        gram_ref[used:, :] = jnp.zeros((gram_ref.shape[0] - used, LANES), jnp.float32)

    half = gram_ref.shape[0] // 2
    quarter = half // n_grp
    keep = pl.multiple_of(core * half, half)
    give = pl.multiple_of((1 - core) * half, half)
    sibling = z * 2 + 1 - core
    first = pltpu.make_async_remote_copy(
        src_ref=gram_ref.at[pl.ds(give, half)], dst_ref=pair_ref,
        send_sem=pair_sems.at[0], recv_sem=pair_sems.at[1],
        device_id={"row": sibling}, device_id_type=MESH,
    )
    first.start()
    for k in range(n_chunk):
        xt_ref[k * chunk:(k + 1) * chunk, :] = x_ref[:, k * chunk:(k + 1) * chunk].T
    first.wait_recv()
    half_ref[...] = gram_ref[pl.ds(keep, half), :] + pair_ref[...]

    second = []
    for s in range(1, n_grp):
        to = lax.rem(grp + s, n_grp)
        copy = pltpu.make_async_remote_copy(
            src_ref=half_ref.at[pl.ds(pl.multiple_of(to * quarter, quarter), quarter)],
            dst_ref=grp_ref.at[grp],
            send_sem=grp_send.at[s], recv_sem=grp_recv.at[s],
            device_id={"grp": to}, device_id_type=MESH,
        )
        copy.start()
        second.append(copy)
    grp_ref[grp] = half_ref[pl.ds(pl.multiple_of(grp * quarter, quarter), quarter), :]
    for copy in second:
        copy.wait_recv()
    z_ref[z] = functools.reduce(lambda a, b: a + b, [grp_ref[g] for g in range(n_grp)])

    third = []
    for s in range(1, n_z):
        to = lax.rem(z + s, n_z)
        copy = pltpu.make_async_remote_copy(
            src_ref=z_ref.at[z], dst_ref=z_ref.at[z],
            send_sem=z_send.at[s], recv_sem=z_recv.at[s],
            device_id={"row": to * 2 + core}, device_id_type=MESH,
        )
        copy.start()
        third.append(copy)
    for copy in third:
        copy.wait_recv()
    sum_ref[core, grp] = functools.reduce(lambda a, b: a + b, [z_ref[i] for i in range(n_z)]) * scale

    fourth = []
    for s in range(1, n_grp):
        to = lax.rem(grp + s, n_grp)
        copy = pltpu.make_async_remote_copy(
            src_ref=sum_ref.at[core, grp], dst_ref=sum_ref.at[core, grp],
            send_sem=back_send.at[s], recv_sem=back_recv.at[s],
            device_id={"grp": to}, device_id_type=MESH,
        )
        copy.start()
        fourth.append(copy)
    for copy in fourth:
        copy.wait_recv()
    last = pltpu.make_async_remote_copy(
        src_ref=sum_ref.at[core], dst_ref=sum_ref.at[core],
        send_sem=back_send.at[0], recv_sem=back_recv.at[0],
        device_id={"row": sibling}, device_id_type=MESH,
    )
    last.start()
    last.wait_recv()
    total_ref[...] = sum_ref[...]

    for k in range(n_chunk):
        for s in steps:
            a2a(k, s).wait_send()
    for copy in [first, *second, *third, *fourth, last]:
        copy.wait_send()


def share(pieces, scale):
    n_row, n_grp = lax.axis_size("row"), lax.axis_size("grp")
    count, depth, width = pieces.shape
    order = depth * n_row
    columns = count * (width // n_row)
    n_chunk = min(4, columns // LANES)
    _, rows = offsets(order)
    quantum = 2 * n_grp * 8
    rows = -(-rows // quantum) * quantum
    quarter = rows // (2 * n_grp)
    n_z = n_row // 2
    f32 = jnp.float32
    dma = pltpu.SemaphoreType.DMA
    vmem = pl.BlockSpec(memory_space=pltpu.VMEM)
    xt, total = pl.pallas_call(
        functools.partial(share_kernel, n_row, n_grp, n_chunk, scale),
        out_shape=[
            jax.ShapeDtypeStruct((columns, order), f32),
            jax.ShapeDtypeStruct((2, n_grp, quarter, LANES), f32),
        ],
        in_specs=[vmem],
        out_specs=[vmem, vmem],
        scratch_shapes=[
            pltpu.VMEM((n_row, depth, columns), f32),
            pltpu.VMEM((order, columns), f32),
            pltpu.VMEM((rows, LANES), f32),
            pltpu.VMEM((rows // 2, LANES), f32),
            pltpu.VMEM((rows // 2, LANES), f32),
            pltpu.VMEM((n_grp, quarter, LANES), f32),
            pltpu.VMEM((n_z, quarter, LANES), f32),
            pltpu.VMEM((2, n_grp, quarter, LANES), f32),
            dma((n_chunk, n_row)), dma((n_chunk, n_row)),
            dma((2,)),
            dma((n_grp,)), dma((n_grp,)),
            dma((n_z,)), dma((n_z,)),
            dma((n_grp,)), dma((n_grp,)),
        ],
        compiler_params=pltpu.CompilerParams(
            collective_id=0, has_side_effects=True, vmem_limit_bytes=48 * 2**20
        ),
    )(pieces)
    return xt, total.reshape(rows, LANES)


def per_device(field):
    fields, third, second, first = field.shape
    count = fields * third * lax.axis_size("grp") * second
    order = first * lax.axis_size("row")
    pieces = jnp.swapaxes(field, 2, 3).reshape(fields * third, first, second)
    xt, packed = share(pieces, 1.0 / count)
    starts, _ = offsets(order)
    blocks = [
        jnp.pad(packed[start:start + order - j * LANES], ((j * LANES, 0), (0, 0)))
        for j, start in enumerate(starts)
    ]
    factor = jnp.linalg.cholesky(jnp.concatenate(blocks, axis=1), symmetrize_input=False)
    solved = lax.linalg.triangular_solve(factor, xt, left_side=False, lower=True, transpose_a=True)
    return (factor, solved.reshape(fields, third, second // lax.axis_size("row"), order))


def solution(mesh):
    return jax.shard_map(
        per_device,
        mesh=mesh,
        in_specs=(P(None, "grp", None, "row"),),
        out_specs=(P(), P(None, "grp", "row", None)),
        check_vma=False,
    )
```

time: 416 us -> 243 us (0.58)
  waiting for transfers between devices: 125 us -> 0 us
  Pallas kernels: 0 us -> 71.9 us
  blocking collectives: 55.3 us -> 0 us
  local copies, waits for them, and re-layouts: 61.6 us -> 15.5 us
  between operations: 17 us -> 3.34 us
  matrix products: 20.8 us -> 13.8 us
    psum x1 -> x0, waiting for transfers between devices: 125 us -> none  [per_device(): total = lax.psum(gram, ('grp', 'row'))]
    pallas_call x0 -> x1, Pallas kernels: none -> 71.9 us  [share(): pl.pallas_call(functools.partial(share_kernel, n_row, n_grp, n_chunk, sca...]
    all_to_all x1 -> x0, blocking collectives: 55.3 us -> none  [per_device(): lax.all_to_all(field, 'row', split_axis=2, concat_axis=3, tiled=True)]
    reshape x2 -> x0, local copies, waits for them, and re-layouts: 18.4 us -> none  [the longest x1 15 us: block_grams(): mats = pieces.reshape(pieces.shape[0], -1, pieces.shape[-1])]
    unnamed x7 -> x2, local copies, waits for them, and re-layouts: 17.5 us -> 1.59 us
    another operation x18, other arithmetic: 121 us -> 134 us  [the longest x14 91.6 us: per_device(): jnp.linalg.cholesky(jnp.concatenate(blocks, axis=1), symmetrize_input=False)]
    all_to_all x1 -> x0, other arithmetic: 7.22 us -> none  [per_device(): lax.all_to_all(field, 'row', split_axis=2, concat_axis=3, tiled=True)]
    all_to_all x2 -> x0, local copies, waits for them, and re-layouts: 7.05 us -> none  [per_device(): lax.all_to_all(field, 'row', split_axis=2, concat_axis=3, tiled=True)]
  transfers between devices with their start and end apart: 1 -> 0, of which waited for: 1 -> 0; matrix products, arithmetic and copies ran while one was open for 1% -> 0% of each run, Pallas kernels for 0% -> 0%
where the time goes in v1:
time: 243 us; the launch traced here: 239 us
  other arithmetic  134 us (55%)
  Pallas kernels  71.9 us (30%)
  local copies, waits for them, and re-layouts  15.5 us (6%)
  matrix products  13.8 us (6%)
  between operations  3.34 us (1%)
    another operation x14, other arithmetic, per_device(): jnp.linalg.cholesky(jnp.concatenate(blocks, axis=1), symmetrize_input=False)  91.6 us
    pallas_call x1, Pallas kernels, share(): pl.pallas_call(functools.partial(share_kernel, n_row, n_grp, n_chunk, sca...  71.9 us
    another operation x4, other arithmetic, per_device(): lax.linalg.triangular_solve(factor, xt, left_side=False, lower=True, tran...  42.7 us
    another operation x12, local copies, waits for them, and re-layouts  10.1 us
    another operation x7, matrix products, per_device(): lax.linalg.triangular_solve(factor, xt, left_side=False, lower=True, tran...  8.14 us
    another operation x6, matrix products, per_device(): jnp.linalg.cholesky(jnp.concatenate(blocks, axis=1), symmetrize_input=False)  5.68 us

profile of v1, /device:TPU:0, one launch (start us, length us, event | category | flops | bytes accessed | tf_op | source)
XLA Modules:
  0.0 238.9 jit_solution(2328780777357290684)
XLA Ops:
  0.7 1.6 copy-done
  2.3 71.9 %shard_map.30 = (f32[1024,512]{1,0:T(8,128)S(1)}, f32[2,4,160,128]{3,2,1,0:T(8,128)S(1)}) custom-call(f32[16,64,512]{2,1,0:T(8,128)S(1)} %bitcast.50), custom_call_target="tpu_custom_call" | custom-call | tf_op jit(solution)/shard_map/pallas_call | solution.py:196
  74.2 11.7 %cholesky.102 = f32[128,128]{1,0:T(8,128)S(1)} custom-call(f32[128,128]{1,0:T(8,128)S(1)} %cholesky.260), custom_call_target="Cholesky" | custom-call | tf_op jit(solution)/shard_map/jit(cholesky)/cholesky | solution.py:237
  85.9 9.8 %custom-call.30 = f32[1,128,128]{1,2,0:T(8,128)S(1)} custom-call(f32[1,128,128]{2,1,0:T(8,128)S(1)} %get-tuple-element.37), custom_call_target="InvertDiagBlocksLowerTriangular" | custom-call | tf_op jit(solution)/shard_map/jit(cholesky)/cholesky | solution.py:237
  95.8 0.7 fusion.18
  97.1 11.7 %cholesky.213 = f32[128,128]{1,0:T(8,128)S(1)} custom-call(f32[128,128]{1,0:T(8,128)S(1)} %cholesky.263), custom_call_target="Cholesky" | custom-call | tf_op jit(solution)/shard_map/jit(cholesky)/cholesky | solution.py:237
  108.8 1.1 cholesky.219
  109.9 0.7 constant_dynamic-update-slice_fusion.3
  110.6 0.6 select_reduce_fusion.2
  111.2 0.7 compare_reduce_fusion.2
  113.1 9.8 %custom-call.31 = f32[1,128,128]{1,2,0:T(8,128)S(1)} custom-call(f32[1,128,128]{2,1,0:T(8,128)S(1)} %get-tuple-element.34), custom_call_target="InvertDiagBlocksLowerTriangular" | custom-call | tf_op jit(solution)/shard_map/jit(cholesky)/cholesky | solution.py:237
  122.9 0.9 convolution_dynamic-update-slice_fusion
  123.8 1.4 convolution_subtract_fusion.3
  125.2 11.7 %cholesky.233 = f32[128,128]{1,0:T(8,128)S(1)} custom-call(f32[128,128]{1,0:T(8,128)S(1)} %cholesky.267), custom_call_target="Cholesky" | custom-call | tf_op jit(solution)/shard_map/jit(cholesky)/cholesky | solution.py:237
  136.9 0.6 select_reduce_fusion.1
  138.7 21.3 %custom-call.32 = f32[1,128,128]{1,2,0:T(8,128)S(1)} custom-call(f32[1,128,128]{2,1,0:T(8,128)S(1)} %get-tuple-element.31), custom_call_target="InvertDiagBlocksLowerTriangular" | custom-call | tf_op jit(solution)/shard_map/jit(cholesky)/cholesky | solution.py:237
  160.0 0.8 convolution_dynamic-update-slice_fusion.1
  160.9 1.4 convolution_subtract_fusion.4
  162.3 11.7 %cholesky.249 = f32[128,128]{1,0:T(8,128)S(1)} custom-call(f32[128,128]{1,0:T(8,128)S(1)} %convolution_subtract_fusion.4), custom_call_target="Cholesky" | custom-call | tf_op jit(solution)/shard_map/jit(cholesky)/cholesky | solution.py:237
  174.0 0.6 select_reduce_fusion
  175.8 2.5 %fusion.12 = (f32[512,512]{1,0:T(8,128)S(1)}, f32[512,512]{1,0:T(8,128)}) fusion(f32[512,512]{1,0:T(8,128)} %get-tuple-element.29, pred[]{:T(512)S(6)} %cholesky.254), kind=kLoop, calls=%fused_computation.22 | loop fusion | flops 1048576 | bytes 3145729 | tf_op jit(solution)/shard_map/triangular_solve | solution.py:238
  178.3 10.1 %while.1 = (s32[]{:T(128)}, f32[512,512]{1,0:T(8,128)S(1)}, s32[4,2]{0,1:T(2,128)S(1)}, f32[4,128,128]{2,1,0:T(8,128)}, s32[]{:T(128)}) while((s32[]{:T(128)}, f32[512,512]{1,0:T(8,128)S(1)}, s32[4,2]{0,1:T(2,128)S(1)}, f32[4,128,128]{2,1,0:T(8,128)}, s32[]{:T(128)}) %tuple.32), condition=%wide.while_cond, body=%wide.while_body.sunk | while | flops 2 | bytes 132205 | solution.py:238
  178.9 1.9 bitcast_dynamic-update-slice_fusion.2
  181.5 1.9 bitcast_dynamic-update-slice_fusion.2
  184.0 1.9 bitcast_dynamic-update-slice_fusion.2
  186.5 1.9 bitcast_dynamic-update-slice_fusion.2
  188.4 40.1 %custom-call.33 = f32[4,128,128]{1,2,0:T(8,128)S(1)} custom-call(f32[4,128,128]{2,1,0:T(8,128)} %get-tuple-element.13), custom_call_target="InvertDiagBlocksLowerTriangular" | custom-call | tf_op jit(solution)/shard_map/triangular_solve | solution.py:238
  228.6 0.6 fusion.13
  229.2 1.0 convolution_subtract_fusion.1
  230.9 1.8 convolution_subtract_fusion
  233.3 2.8 %fusion.6 = f32[1024,128]{1,0:T(8,128)S(1)} fusion(f32[1024,128]{0,1:T(8,128)S(1)} %fusion.24, f32[1024,128]{0,1:T(8,128)S(1)} %fusion.25, f32[1024,128]{0,1:T(8,128)S(1)} %bitcast.57, f32[1024,512]{1,0:T(8,128)S(1)} %get-tuple-element.5, f32[512,512]{1,0:T(8,128)S(1)} %get-tuple-element.84), kind=kOutput, calls=%fused_computation.10 | convolution fusion | flops 604897280 | bytes 2818048 | tf_op jit(solution)/shard_map/triangular_solve | solution.py:238
  236.9 1.8 copy.6
  (24 shorter events, 6.4 us)
Async XLA Ops:
  0.7 1.6 copy-start

commit v2 on v1

--- a/solution.py
+++ b/solution.py
@@ -223,19 +223,127 @@
     return xt, total.reshape(rows, LANES)
 
 
+def eliminate(work_ref, upper_ref, inverse_ref):
+    sub = lax.broadcasted_iota(jnp.int32, (8, LANES), 0)
+    full = (8, LANES)
+
+    def splat_rows(value):
+        return [jnp.broadcast_to(value[i:i + 1, :], full) for i in range(8)]
+
+    def gather_rows(rows):
+        out = rows[0]
+        for i in range(1, 8):
+            out = jnp.where(sub == i, rows[i], out)
+        return out
+
+    for j in range(LANES // 8):
+        at = 8 * j
+        left = work_ref[at:at + 8, :LANES]
+        right = work_ref[at:at + 8, LANES:]
+        d = [[None] * 8 for _ in range(8)]
+        for m in range(8):
+            spread = jnp.broadcast_to(left[:, at + m:at + m + 1], full)
+            for i in range(m, 8):
+                d[i][m] = jnp.broadcast_to(spread[i:i + 1, :], full)
+        a = splat_rows(left)
+        e = splat_rows(right)
+        inv = [None] * 8
+        for k in range(8):
+            inv[k] = lax.rsqrt(d[k][k])
+            for i in range(k + 1, 8):
+                d[i][k] = d[i][k] * inv[k]
+            for m in range(k + 1, 8):
+                for i in range(m, 8):
+                    d[i][m] = d[i][m] - d[i][k] * d[m][k]
+            a[k] = a[k] * inv[k]
+            e[k] = e[k] * inv[k]
+            for i in range(k + 1, 8):
+                a[i] = a[i] - d[i][k] * a[k]
+                e[i] = e[i] - d[i][k] * e[k]
+        upper_ref[at:at + 8, :] = gather_rows(a)
+        inverse_ref[at:at + 8, :] = gather_rows(e)
+        for k in reversed(range(8)):
+            a[k] = a[k] * inv[k]
+            e[k] = e[k] * inv[k]
+            for i in range(k):
+                a[i] = a[i] - d[k][i] * a[k]
+                e[i] = e[i] - d[k][i] * e[k]
+        for g in range(j + 1, LANES // 8):
+            left = work_ref[8 * g:8 * g + 8, :LANES]
+            right = work_ref[8 * g:8 * g + 8, LANES:]
+            spreads = [jnp.broadcast_to(left[:, at + k:at + k + 1], full) for k in range(8)]
+            for k in range(8):
+                left = left - spreads[k] * a[k]
+                right = right - spreads[k] * e[k]
+            work_ref[8 * g:8 * g + 8, :LANES] = left
+            work_ref[8 * g:8 * g + 8, LANES:] = right
+
+
+def solve_kernel(total_ref, xt_ref, factor_ref, out_ref, gram_ref, work_ref, upper_ref, inverse_ref):
+    order = factor_ref.shape[0]
+    starts, used = offsets(order)
+    dot = functools.partial(
+        lax.dot_general, dimension_numbers=NT, precision=HIGHEST, preferred_element_type=jnp.float32
+    )
+    r = lax.broadcasted_iota(jnp.int32, (LANES, LANES), 0)
+    c = lax.broadcasted_iota(jnp.int32, (LANES, LANES), 1)
+    blocks = order // LANES
+    gram_ref[...] = total_ref[:used, :]
+    for b in range(blocks):
+        lo, hi = b * LANES, (b + 1) * LANES
+        start = starts[b]
+        work_ref[b, :, :LANES] = gram_ref[start:start + LANES, :]
+        work_ref[b, :, LANES:] = jnp.where(r == c, 1.0, 0.0)
+        eliminate(work_ref.at[b], upper_ref.at[b], inverse_ref.at[b])
+        inverse = inverse_ref[b]
+        if hi < order:
+            below = dot(gram_ref[start + LANES:start + order - lo, :], inverse)
+            factor_ref[hi:, lo:hi] = below
+            for j in range(b + 1, blocks):
+                skip = (j - b - 1) * LANES
+                here = slice(starts[j], starts[j] + order - j * LANES)
+                gram_ref[here, :] -= dot(below[skip:, :], below[skip:skip + LANES, :])
+        factor_ref[lo:hi, lo:hi] = jnp.where(r >= c, upper_ref[b].T, 0.0)
+        if b:
+            factor_ref[:lo, lo:hi] = jnp.zeros((lo, LANES), jnp.float32)
+        source = xt_ref if b == 0 else out_ref
+        solved = dot(source[:, lo:hi], inverse)
+        out_ref[:, lo:hi] = solved
+        if hi < order:
+            out_ref[:, hi:] = source[:, hi:] - dot(solved, below)
+
+
+def factor_and_solve(packed, xt):
+    columns, order = xt.shape
+    _, used = offsets(order)
+    f32 = jnp.float32
+    blocks = order // LANES
+    vmem = pl.BlockSpec(memory_space=pltpu.VMEM)
+    return pl.pallas_call(
+        solve_kernel,
+        out_shape=[
+            jax.ShapeDtypeStruct((order, order), f32),
+            jax.ShapeDtypeStruct((columns, order), f32),
+        ],
+        in_specs=[vmem, vmem],
+        out_specs=[vmem, vmem],
+        scratch_shapes=[
+            pltpu.VMEM((used, LANES), f32),
+            pltpu.VMEM((blocks, LANES, 2 * LANES), f32),
+            pltpu.VMEM((blocks, LANES, LANES), f32),
+            pltpu.VMEM((blocks, LANES, LANES), f32),
+        ],
+        compiler_params=pltpu.CompilerParams(vmem_limit_bytes=48 * 2**20),
+    )(packed, xt)
+
+
 def per_device(field):
     fields, third, second, first = field.shape
     count = fields * third * lax.axis_size("grp") * second
     order = first * lax.axis_size("row")
     pieces = jnp.swapaxes(field, 2, 3).reshape(fields * third, first, second)
     xt, packed = share(pieces, 1.0 / count)
-    starts, _ = offsets(order)
-    blocks = [
-        jnp.pad(packed[start:start + order - j * LANES], ((j * LANES, 0), (0, 0)))
-        for j, start in enumerate(starts)
-    ]
-    factor = jnp.linalg.cholesky(jnp.concatenate(blocks, axis=1), symmetrize_input=False)
-    solved = lax.linalg.triangular_solve(factor, xt, left_side=False, lower=True, transpose_a=True)
+    factor, solved = factor_and_solve(packed, xt)
     return (factor, solved.reshape(fields, third, second // lax.axis_size("row"), order))
 
 

time: 243 us -> 99.6 us (0.41); the launches traced: 239 us -> 99.1 us
  other arithmetic: 134 us -> 0 us
  Pallas kernels: 71.9 us -> 96.9 us
  local copies, waits for them, and re-layouts: 15.5 us -> 1.58 us
  matrix products: 13.8 us -> 0 us
  between operations: 3.34 us -> 0.65 us
    another operation x18 -> x0, other arithmetic: 134 us -> none  [the longest x14 91.6 us: per_device(): jnp.linalg.cholesky(jnp.concatenate(blocks, axis=1), symmetrize_input=False)]
    pallas_call x0 -> x1, Pallas kernels: none -> 25 us  [factor_and_solve(): pl.pallas_call(solve_kernel, out_shape=[jax.ShapeDtypeStruct((order, orde...]
    another operation x20 -> x0, local copies, waits for them, and re-layouts: 13.9 us -> none
    another operation x13 -> x0, matrix products: 13.8 us -> none  [the longest x7 8.14 us: per_device(): lax.linalg.triangular_solve(factor, xt, left_side=False, lower=True, tran...]
where the time goes in v2:
time: 99.6 us; the launch traced here: 99.1 us
  Pallas kernels  96.9 us (97%)
  local copies, waits for them, and re-layouts  1.58 us (2%)
    pallas_call x1, Pallas kernels, share(): pl.pallas_call(functools.partial(share_kernel, n_row, n_grp, n_chunk, sca...  71.9 us
    pallas_call x1, Pallas kernels, factor_and_solve(): pl.pallas_call(solve_kernel, out_shape=[jax.ShapeDtypeStruct((order, orde...  25 us

profile of v2, /device:TPU:0, one launch (start us, length us, event | category | flops | bytes accessed | tf_op | source)
XLA Modules:
  0.0 99.1 jit_solution(12681204907464706303)
XLA Ops:
  0.6 0.0 copy-start
  0.6 1.6 %copy-done = f32[4,4,512,64]{2,3,1,0:T(8,128)S(1)} copy-done((f32[4,4,512,64]{2,3,1,0:T(8,128)S(1)}, f32[4,4,512,64]{2,3,1,0:T(8,128)}, u32[]{:S(2)}) %copy-start) | copy-done | bytes 2097176
  2.2 71.9 %shard_map.30 = (f32[1024,512]{1,0:T(8,128)S(1)}, f32[2,4,160,128]{3,2,1,0:T(8,128)S(1)}) custom-call(f32[16,64,512]{2,1,0:T(8,128)S(1)} %bitcast.5), custom_call_target="tpu_custom_call" | custom-call | tf_op jit(solution)/shard_map/pallas_call | solution.py:196
  74.1 25.0 %shard_map.31 = (f32[512,512]{1,0:T(8,128)}, f32[1024,512]{1,0:T(8,128)}) custom-call(f32[1280,128]{1,0:T(8,128)S(1)} %bitcast.6, f32[1024,512]{1,0:T(8,128)S(1)} %get-tuple-element.7.xt_ref), custom_call_target="tpu_custom_call" | custom-call | tf_op jit(solution)/shard_map/pallas_call | solution.py:322
Async XLA Ops:
  0.6 1.6 %copy-start = (f32[4,4,512,64]{2,3,1,0:T(8,128)S(1)}, f32[4,4,512,64]{2,3,1,0:T(8,128)}, u32[]{:S(2)}) copy-start(f32[4,4,512,64]{2,3,1,0:T(8,128)} %param.1) | copy-start | bytes 6291460

commit v3 on v2

--- a/solution.py
+++ b/solution.py
@@ -223,12 +223,9 @@
     return xt, total.reshape(rows, LANES)
 
 
-def eliminate(work_ref, upper_ref, inverse_ref):
+def eliminate(work_ref, upper_ref, inverse_ref, spread_ref):
     sub = lax.broadcasted_iota(jnp.int32, (8, LANES), 0)
     full = (8, LANES)
-
-    def splat_rows(value):
-        return [jnp.broadcast_to(value[i:i + 1, :], full) for i in range(8)]
 
     def gather_rows(rows):
         out = rows[0]
@@ -236,18 +233,31 @@
             out = jnp.where(sub == i, rows[i], out)
         return out
 
-    for j in range(LANES // 8):
+    def update(g, at, a, e):
+        left = work_ref[8 * g:8 * g + 8, :LANES]
+        right = work_ref[8 * g:8 * g + 8, LANES:]
+        spreads = [jnp.broadcast_to(left[:, at + k:at + k + 1], full) for k in range(8)]
+        for k in range(8):
+            left = left - spreads[k] * a[k]
+            right = right - spreads[k] * e[k]
+        work_ref[8 * g:8 * g + 8, :LANES] = left
+        work_ref[8 * g:8 * g + 8, LANES:] = right
+
+    pending = []
+    groups = LANES // 8
+    for j in range(groups):
         at = 8 * j
         left = work_ref[at:at + 8, :LANES]
-        right = work_ref[at:at + 8, LANES:]
         d = [[None] * 8 for _ in range(8)]
         for m in range(8):
             spread = jnp.broadcast_to(left[:, at + m:at + m + 1], full)
+            spread_ref[j % 2, 8 * m:8 * m + 8, :] = spread
             for i in range(m, 8):
-                d[i][m] = jnp.broadcast_to(spread[i:i + 1, :], full)
-        a = splat_rows(left)
-        e = splat_rows(right)
+                d[i][m] = jnp.broadcast_to(spread_ref[j % 2, 8 * m + i:8 * m + i + 1, :], full)
+        a = [jnp.broadcast_to(work_ref[at + i:at + i + 1, :LANES], full) for i in range(8)]
+        e = [jnp.broadcast_to(work_ref[at + i:at + i + 1, LANES:], full) for i in range(8)]
         inv = [None] * 8
+        share_of = -(-len(pending) // 8)
         for k in range(8):
             inv[k] = lax.rsqrt(d[k][k])
             for i in range(k + 1, 8):
@@ -260,6 +270,8 @@
             for i in range(k + 1, 8):
                 a[i] = a[i] - d[i][k] * a[k]
                 e[i] = e[i] - d[i][k] * e[k]
+            for step in pending[k * share_of:(k + 1) * share_of]:
+                update(*step)
         upper_ref[at:at + 8, :] = gather_rows(a)
         inverse_ref[at:at + 8, :] = gather_rows(e)
         for k in reversed(range(8)):
@@ -268,18 +280,22 @@
             for i in range(k):
                 a[i] = a[i] - d[k][i] * a[k]
                 e[i] = e[i] - d[k][i] * e[k]
-        for g in range(j + 1, LANES // 8):
-            left = work_ref[8 * g:8 * g + 8, :LANES]
-            right = work_ref[8 * g:8 * g + 8, LANES:]
-            spreads = [jnp.broadcast_to(left[:, at + k:at + k + 1], full) for k in range(8)]
-            for k in range(8):
-                left = left - spreads[k] * a[k]
-                right = right - spreads[k] * e[k]
-            work_ref[8 * g:8 * g + 8, :LANES] = left
-            work_ref[8 * g:8 * g + 8, LANES:] = right
-
-
-def solve_kernel(total_ref, xt_ref, factor_ref, out_ref, gram_ref, work_ref, upper_ref, inverse_ref):
+        end = groups // 2 if j < groups // 2 else groups
+        if j + 1 < end:
+            update(j + 1, at, a, e)
+        pending = [(g, at, tuple(a), tuple(e)) for g in range(j + 2, end)]
+        if j + 1 == groups // 2:
+            cut = LANES // 2
+            turned = upper_ref[:cut, :].T[cut:, :]
+            work_ref[cut:, :LANES] -= jnp.dot(
+                turned, upper_ref[:cut, :], precision=HIGHEST, preferred_element_type=jnp.float32
+            )
+            work_ref[cut:, LANES:] -= jnp.dot(
+                turned, inverse_ref[:cut, :], precision=HIGHEST, preferred_element_type=jnp.float32
+            )
+
+
+def solve_kernel(total_ref, xt_ref, factor_ref, out_ref, gram_ref, work_ref, upper_ref, inverse_ref, spread_ref):
     order = factor_ref.shape[0]
     starts, used = offsets(order)
     dot = functools.partial(
@@ -294,15 +310,18 @@
         start = starts[b]
         work_ref[b, :, :LANES] = gram_ref[start:start + LANES, :]
         work_ref[b, :, LANES:] = jnp.where(r == c, 1.0, 0.0)
-        eliminate(work_ref.at[b], upper_ref.at[b], inverse_ref.at[b])
+        eliminate(work_ref.at[b], upper_ref.at[b], inverse_ref.at[b], spread_ref)
         inverse = inverse_ref[b]
         if hi < order:
-            below = dot(gram_ref[start + LANES:start + order - lo, :], inverse)
-            factor_ref[hi:, lo:hi] = below
-            for j in range(b + 1, blocks):
-                skip = (j - b - 1) * LANES
-                here = slice(starts[j], starts[j] + order - j * LANES)
-                gram_ref[here, :] -= dot(below[skip:, :], below[skip:skip + LANES, :])
+            below = []
+            for i in range(b + 1, blocks):
+                here = start + (i - b) * LANES
+                part = dot(gram_ref[here:here + LANES, :], inverse)
+                factor_ref[i * LANES:(i + 1) * LANES, lo:hi] = part
+                below.append(part)
+                for j in range(b + 1, i + 1):
+                    here = starts[j] + (i - j) * LANES
+                    gram_ref[here:here + LANES, :] -= dot(part, below[j - b - 1])
         factor_ref[lo:hi, lo:hi] = jnp.where(r >= c, upper_ref[b].T, 0.0)
         if b:
             factor_ref[:lo, lo:hi] = jnp.zeros((lo, LANES), jnp.float32)
@@ -310,7 +329,9 @@
         solved = dot(source[:, lo:hi], inverse)
         out_ref[:, lo:hi] = solved
         if hi < order:
-            out_ref[:, hi:] = source[:, hi:] - dot(solved, below)
+            for j in range(b + 1, blocks):
+                there = slice(j * LANES, (j + 1) * LANES)
+                out_ref[:, there] = source[:, there] - dot(solved, below[j - b - 1])
 
 
 def factor_and_solve(packed, xt):
@@ -332,6 +353,7 @@
             pltpu.VMEM((blocks, LANES, 2 * LANES), f32),
             pltpu.VMEM((blocks, LANES, LANES), f32),
             pltpu.VMEM((blocks, LANES, LANES), f32),
+            pltpu.VMEM((2, 64, LANES), f32),
         ],
         compiler_params=pltpu.CompilerParams(vmem_limit_bytes=48 * 2**20),
     )(packed, xt)

time: 99.6 us -> 96.1 us (0.965)
  Pallas kernels: 96.9 us -> 93.4 us
    pallas_call x1, Pallas kernels: 25 us -> 21.5 us  [factor_and_solve(): pl.pallas_call(solve_kernel, out_shape=[jax.ShapeDtypeStruct((order, orde...]
where the time goes in v3:
time: 96.1 us; the launch traced here: 95.6 us
  Pallas kernels  93.4 us (97%)
  local copies, waits for them, and re-layouts  1.58 us (2%)
    pallas_call x1, Pallas kernels, share(): pl.pallas_call(functools.partial(share_kernel, n_row, n_grp, n_chunk, sca...  71.9 us
    pallas_call x1, Pallas kernels, factor_and_solve(): pl.pallas_call(solve_kernel, out_shape=[jax.ShapeDtypeStruct((order, orde...  21.5 us

profile of v3, /device:TPU:0, one launch (start us, length us, event | category | flops | bytes accessed | tf_op | source)
XLA Modules:
  0.0 95.6 jit_solution(3010770653365556184)
XLA Ops:
  0.6 0.0 copy-start
  0.6 1.6 %copy-done = f32[4,4,512,64]{2,3,1,0:T(8,128)S(1)} copy-done((f32[4,4,512,64]{2,3,1,0:T(8,128)S(1)}, f32[4,4,512,64]{2,3,1,0:T(8,128)}, u32[]{:S(2)}) %copy-start) | copy-done | bytes 2097176
  2.2 71.9 %shard_map.30 = (f32[1024,512]{1,0:T(8,128)S(1)}, f32[2,4,160,128]{3,2,1,0:T(8,128)S(1)}) custom-call(f32[16,64,512]{2,1,0:T(8,128)S(1)} %bitcast.5), custom_call_target="tpu_custom_call" | custom-call | tf_op jit(solution)/shard_map/pallas_call | solution.py:196
  74.1 21.5 %shard_map.31 = (f32[512,512]{1,0:T(8,128)}, f32[1024,512]{1,0:T(8,128)}) custom-call(f32[1280,128]{1,0:T(8,128)S(1)} %bitcast.6, f32[1024,512]{1,0:T(8,128)S(1)} %get-tuple-element.7.xt_ref), custom_call_target="tpu_custom_call" | custom-call | tf_op jit(solution)/shard_map/pallas_call | solution.py:343
Async XLA Ops:
  0.6 1.6 %copy-start = (f32[4,4,512,64]{2,3,1,0:T(8,128)S(1)}, f32[4,4,512,64]{2,3,1,0:T(8,128)}, u32[]{:S(2)}) copy-start(f32[4,4,512,64]{2,3,1,0:T(8,128)} %param.1) | copy-start | bytes 6291460
